TPU v7x, 32 devices: a whole 2x2x4 slice. The times are simulated.
32 devices in a mesh: groups: 2 (over y), site: 4 (over z), sample: 4 (over x, core).
Axes of the slice: x: 2, y: 2, z: 4, core: 2. Of those that a mesh axis runs over, the one named last changes fastest.
Arguments:
- site_tensor: bfloat16 [8, 2048, 2, 2048], P(('groups', 'site'), None, None, 'sample'), parts along dimension 0, may hold values from -0.25 to 0.25
- fronts_in: bfloat16 [3072, 2048], P(('groups', 'sample')), parts along dimension 0
- outcomes: int32 [8, 1536], P(('groups', 'site'), 'sample'), parts along dimension 0, may hold values from 0 to 1
- charges: int32 [10, 16], P('groups'), parts along dimension 0, may hold values from 0 to 3
Outputs:
- fronts_out: bfloat16 [8, 1536, 2048], P(('groups', 'site'), 'sample'), parts along dimension 0
- log_steps: float32 [8, 1536], P(('groups', 'site'), 'sample'), parts along dimension 0
There are 2 independent parts, one for each index of `groups`. A program takes and returns all parts, laid end to end along the dimension named above; each array names one. Nothing has to cross between parts.
All inputs are finite; a program needn't handle non-finite values.
Results may differ from a plain program's by a relative error of at most 0.012.
Values may be sent and summed in bfloat16 or wider, within the bound.
A program may use at most 128 MiB of HBM per device.

v0:
```python
import functools

import jax
import jax.numpy as jnp
from jax import lax
from jax.experimental import pallas as pl
from jax.experimental.pallas import tpu as pltpu
from jax.sharding import PartitionSpec as P

BLOCK = 128
CHARGES = 4
PHYS = 2
LANES = 128
SUB = 16
MESH = pl.DeviceIdType.MESH

epsilon = 1e-06


def chain_kernel(
    chips, sites, micro, pieces, tensor_ref, charges_ref, fronts_ref, picks_ref,
    out_ref, log_ref,
    wf, wx, merged, landed, full, acc, sums, ybuf, gath, marks, columns, logs,
    x_send, x_recv, s_send, s_recv, z_send, z_recv, a_send, a_recv, p_send, p_recv,
    w_send, w_recv, b_send, b_recv,
):
    samples = 2 * chips
    site = lax.axis_index("site")
    me = lax.axis_index("sample")
    chip, core = me // 2, lax.rem(me, 2)
    sibling = chip * 2 + (1 - core)
    _, bond, cols = tensor_ref.shape
    rows = fronts_ref.shape[0]
    steps = rows // micro
    pair = 2 * micro
    depth = bond // pieces
    tail = sites - 1
    is_tail, is_body = site == tail, site != tail

    def ahead(d):
        return lax.rem(chip + d, chips) * 2 + core

    def behind(d, which):
        return lax.rem(chip + chips - d, chips) * 2 + which

    barrier = pltpu.get_barrier_semaphore()
    for e in range(1, samples):
        pl.semaphore_signal(
            barrier, inc=1, device_id={"sample": lax.rem(me + e, samples)}, device_id_type=MESH
        )

    @pl.when(site > 0)
    def _():
        pl.semaphore_signal(barrier, inc=1, device_id={"site": site - 1}, device_id_type=MESH)

    @pl.when(site < sites - 1)
    def _():
        pl.semaphore_signal(barrier, inc=1, device_id={"site": site + 1}, device_id_type=MESH)

    ends = jnp.where(site > 0, 1, 0) + jnp.where(site < sites - 1, 1, 0)
    pl.semaphore_wait(barrier, samples - 1 + ends)

    def remote(src, dst, sent, got, target):
        return pltpu.make_async_remote_copy(
            src_ref=src, dst_ref=dst, send_sem=sent, recv_sem=got,
            device_id=target, device_id_type=MESH,
        )

    def by_rows(owner, b, to):
        return full.at[:, b, pl.ds(pl.multiple_of(owner * micro, SUB), micro), :]

    def by_columns(owner, b, to):
        return full.at[owner, b]

    def by_chip(owner, b, to):
        return full.at[owner, b, pl.ds(pl.multiple_of(to * pair, SUB), pair), :]

    def each(act):
        @pl.when(site == 0)
        def _():
            act(by_rows)

        @pl.when((site > 0) & (site < tail))
        def _():
            act(by_columns)

        @pl.when(is_tail)
        def _():
            act(by_chip)

    def x_copy(block, owner, d, b, to):
        part = block(owner, b, to)
        return remote(
            part, part, x_send.at[d - 1, b], x_recv.at[d - 1, b], {"sample": ahead(d)}
        )

    def s_copy(block, owner, d, b):
        part = block(owner, b, chip)
        return remote(part, part, s_send.at[d, b], s_recv.at[d, b], {"sample": sibling})

    def w_copy(d, c):
        span = pl.ds(c * depth, depth)
        return remote(
            merged.at[span, :], landed.at[d - 1, span, :],
            w_send.at[d - 1, c], w_recv.at[d - 1, c], {"sample": ahead(d)},
        )

    def t_rows(d, b, which):
        at = pl.multiple_of(d * pair + which * micro, SUB)
        return pl.ds(at, micro)

    def t_copy(d, b):
        return remote(
            ybuf.at[b, t_rows(d, b, 1 - core), :], gath.at[behind(d, core), b],
            a_send.at[d, b], a_recv.at[d, b], {"sample": sibling},
        )

    def t_arrival(d, b):
        slot = gath.at[behind(d, 1 - core), b]
        return remote(slot, slot, a_send.at[d, b], a_recv.at[d, b], {"sample": sibling})

    def z_copy(b):
        return remote(
            ybuf.at[b], full.at[me, b], z_send.at[b], z_recv.at[b],
            {"site": jnp.minimum(site + 1, sites - 1)},
        )

    def b_copy(b):
        return remote(
            full.at[:, b, pl.ds(pl.multiple_of(me * micro, SUB), micro), :],
            gath.at[:, b], b_send.at[b], b_recv.at[b],
            {"site": jnp.maximum(site - 1, 0)},
        )

    def p_copy(e):
        target = lax.rem(me + e, samples)
        return remote(
            marks.at[me], marks.at[me], p_send.at[e - 1], p_recv.at[e - 1], {"sample": target}
        )

    def p_arrival(e):
        source = lax.rem(me + samples - e, samples)
        return remote(
            marks.at[source], marks.at[source],
            p_send.at[e - 1], p_recv.at[e - 1], {"sample": source},
        )

    def launch(b):
        def act(block):
            for d in range(1, chips):
                x_copy(block, me, d, b, lax.rem(chip + d, chips)).start()
            s_copy(block, me, 0, b).start()

        each(act)

    marks[me] = jnp.broadcast_to(picks_ref[...].astype(jnp.float32), (8, rows))
    for e in range(1, samples):
        p_copy(e).start()

    @pl.when(site == 0)
    def _():
        for b in range(steps):
            for o in range(samples):
                full[o, b, pl.ds(pl.multiple_of(me * micro, SUB), micro), :] = fronts_ref[
                    b * micro : (b + 1) * micro, o * cols : (o + 1) * cols
                ]
        launch(0)

    def expand(owner, load, save, first, last):
        def body(i, carry):
            left = charges_ref[site, i]
            here = cols // BLOCK
            part, inner = i // here, lax.rem(i, here) * BLOCK
            for j in range(cols // BLOCK):
                right = charges_ref[site + 1, owner * (cols // BLOCK) + j]
                allowed = []
                for p in range(PHYS):
                    fits = jnp.where(right == lax.rem(left + p, CHARGES), 1.0, 0.0)
                    allowed.append(jnp.full((SUB, BLOCK), fits, jnp.float32).astype(jnp.bfloat16))
                lanes = slice(j * BLOCK, (j + 1) * BLOCK)
                for u in range(BLOCK // SUB):
                    at = pl.multiple_of(i * BLOCK + u * SUB, SUB)
                    to = (part, pl.multiple_of(inner + u * SUB, SUB))
                    save(to, at, lanes, [load(p, at, lanes) * allowed[p] for p in range(PHYS)])
            return carry

        lax.fori_loop(first, last, body, 0)

    def load_own(p, at, lanes):
        return tensor_ref[p, pl.ds(at, SUB), lanes]

    def save_own(to, at, lanes, values):
        for p in range(PHYS):
            wf[to[0], pl.ds(p * cols + to[1], SUB), lanes] = values[p]

    def save_tail(to, at, lanes, values):
        save_own(to, at, lanes, values)
        merged[pl.ds(at, SUB), lanes] = values[0] + values[1]

    per = depth // BLOCK

    @pl.when(is_body)
    def _():
        expand(me, load_own, save_own, 0, bond // BLOCK)

    @pl.when(is_tail)
    def _():
        for c in range(pieces):
            expand(me, load_own, save_tail, c * per, (c + 1) * per)
            for d in range(1, chips):
                w_copy(d, c).start()

    for e in range(1, samples):
        p_arrival(e).wait_recv()
    for o in range(samples):
        for j in range(rows // LANES):
            line = marks[o, 0:1, j * LANES : (j + 1) * LANES]
            square = jnp.broadcast_to(line, (LANES, LANES)).T.astype(jnp.bfloat16)
            for q in range(LANES // micro):
                columns[j * (LANES // micro) + q, o * micro : (o + 1) * micro, :] = square[
                    q * micro : (q + 1) * micro, :
                ]

    @pl.when(is_tail)
    def _():
        for c in range(pieces):
            for d in range(1, chips):
                w_copy(d, c).wait_recv()

                def load_far(p, at, lanes):
                    return landed[d - 1, pl.ds(at, SUB), lanes]

                def save_far(to, at, lanes, values):
                    for p in range(PHYS):
                        wx[d - 1, to[0], pl.ds(p * cols + to[1], SUB), lanes] = values[p]

                expand(behind(d, core), load_far, save_far, c * per, (c + 1) * per)

    @pl.when(site > 0)
    def _():
        z_copy(0).wait_recv()
        launch(0)

    first = jnp.where(site == 0, 1.0, 0.0)

    chip_rows = pl.ds(pl.multiple_of(chip * pair, SUB), pair)

    def contract(b, c, start, last):
        if last:
            front, picks, count = full[c, b, chip_rows, :], columns[b, chip_rows, :], pair
        else:
            front, picks, count = full[c, b], columns[b], samples * micro
        second = front * jnp.concatenate([picks] * (cols // LANES), axis=1)
        both = jnp.concatenate([front - second, second], axis=1)
        total = jnp.zeros((count, LANES), jnp.float32)
        for k in range(cols // LANES):
            wide = front[:, k * LANES : (k + 1) * LANES].astype(jnp.float32)
            total = total + wide * wide
        sums[0:count, :] = total if start else sums[0:count, :] + total
        for d in range(chips if last else 1):
            right = wf[c] if d == 0 else wx[d - 1, c]
            part = jnp.dot(both, right, preferred_element_type=jnp.float32)
            acc[d, 0:count, :] = part if start else acc[d, 0:count, :] + part

    def scale_of(count):
        mean = jnp.sum(sums[0:count, :], axis=1, keepdims=True) * (1.0 / bond)
        inverse = 1.0 / jnp.sqrt(mean + epsilon)
        return inverse + first * (1.0 - inverse)

    def finish(b):
        total = jnp.zeros((micro, LANES), jnp.float32)
        for c in range(samples):
            for k in range(cols // LANES):
                wide = gath[c, b, :, k * LANES : (k + 1) * LANES].astype(jnp.float32)
                total = total + wide * wide
        norm = jnp.sqrt(jnp.sum(total, axis=1, keepdims=True) * (1.0 / bond) + epsilon)
        inverse = 1.0 / norm
        span = pl.ds(pl.multiple_of(b * micro, SUB), micro)
        logs[span, :] = jnp.broadcast_to(jnp.log(norm), (micro, LANES))
        for c in range(samples):
            wide = gath[c, b].astype(jnp.float32)
            out_ref[span, c * cols : (c + 1) * cols] = (wide * inverse).astype(jnp.bfloat16)

    def finish_body(b, carry):
        b_copy(b).wait_recv()
        finish(b)
        return carry

    def finish_tail(b):
        for d in range(chips):
            t_arrival(d, b).wait_recv()
        finish(b)

    def early(b, block, last):
        contract(b, me, True, last)
        s_copy(block, sibling, 0, b).wait_recv()
        contract(b, sibling, False, last)

    def late(b, block, last):
        for d in range(1, chips):
            x_copy(block, behind(d, core), d, b, chip).wait_recv()
            s_copy(block, behind(d, core), d, b).start()
            contract(b, behind(d, core), False, last)
            s_copy(block, behind(d, 1 - core), d, b).wait_recv()
            contract(b, behind(d, 1 - core), False, last)

    def step(b, carry):
        @pl.when((site > 0) & (site < tail))
        def _():
            early(b, by_columns, False)

        @pl.when(is_tail)
        def _():
            early(b, by_chip, True)

        @pl.when(b + 1 < steps)
        def _():
            @pl.when(site > 0)
            def _():
                z_copy(b + 1).wait_recv()

            launch(b + 1)

        @pl.when(site == 0)
        def _():
            for d in range(1, chips):
                x_copy(by_rows, behind(d, core), d, b, chip).wait_recv()
                s_copy(by_rows, behind(d, core), d, b).start()
            for d in range(chips):
                s_copy(by_rows, behind(d, 1 - core), d, b).wait_recv()
            for c in range(samples):
                contract(b, c, c == 0, False)

        @pl.when((site > 0) & (site < tail))
        def _():
            late(b, by_columns, False)

        @pl.when(is_tail)
        def _():
            late(b, by_chip, True)

        @pl.when(is_body)
        def _():
            ybuf[b] = (acc[0] * scale_of(samples * micro)).astype(jnp.bfloat16)
            z_copy(b).start()

        @pl.when(is_tail)
        def _():
            scale = scale_of(pair)
            for d in range(chips):
                ybuf[b, d * pair : (d + 1) * pair, :] = (acc[d, 0:pair, :] * scale).astype(
                    jnp.bfloat16
                )
                t_copy(d, b).start()
                gath[behind(d, core), b] = ybuf[b, t_rows(d, b, core), :]

        @pl.when(site > 0)
        def _():
            b_copy(b).start()

        @pl.when(is_tail & (b > 0))
        def _():
            finish_tail(b - 1)

        return carry

    lax.fori_loop(0, steps, step, 0)

    @pl.when(is_tail)
    def _():
        finish_tail(steps - 1)

    @pl.when(is_body)
    def _():
        lax.fori_loop(0, steps, finish_body, 0)

    for j in range(rows // LANES):
        square = logs[j * LANES : (j + 1) * LANES, :].T
        log_ref[0:1, j * LANES : (j + 1) * LANES] = square[0:1, :]

    for e in range(1, samples):
        p_copy(e).wait_send()

    @pl.when(is_tail)
    def _():
        for c in range(pieces):
            for d in range(1, chips):
                w_copy(d, c).wait_send()

    def drain(b, carry):
        def act(block):
            for d in range(1, chips):
                x_copy(block, me, d, b, lax.rem(chip + d, chips)).wait_send()
            for d in range(chips):
                s_copy(block, behind(d, core), d, b).wait_send()

        each(act)

        @pl.when(site > 0)
        def _():
            b_copy(b).wait_send()

        @pl.when(is_tail)
        def _():
            for d in range(chips):
                t_copy(d, b).wait_send()

        @pl.when(site < sites - 1)
        def _():
            z_copy(b).wait_send()

        return carry

    lax.fori_loop(0, steps, drain, 0)


def per_device(site_tensor, fronts_in, outcomes, charges):
    sites = lax.axis_size("site")
    samples = lax.axis_size("sample")
    chips = samples // 2
    _, bond, _, cols = site_tensor.shape
    rows = fronts_in.shape[0]
    tensor = site_tensor[0].transpose(1, 0, 2)
    pieces = 4

    micro = 32
    steps = rows // micro
    vmem = pl.BlockSpec(memory_space=pltpu.VMEM)
    dma = pltpu.SemaphoreType.DMA
    peers = max(chips - 1, 1)
    fronts, logs = pl.pallas_call(
        functools.partial(chain_kernel, chips, sites, micro, pieces),
        out_shape=(
            jax.ShapeDtypeStruct((rows, bond), jnp.bfloat16),
            jax.ShapeDtypeStruct((1, rows), jnp.float32),
        ),
        in_specs=[vmem, pl.BlockSpec(memory_space=pltpu.SMEM), vmem, vmem],
        out_specs=(vmem, vmem),
        scratch_shapes=[
            pltpu.VMEM((samples, PHYS * cols, cols), jnp.bfloat16),
            pltpu.VMEM((peers, samples, PHYS * cols, cols), jnp.bfloat16),
            pltpu.VMEM((bond, cols), jnp.bfloat16),
            pltpu.VMEM((peers, bond, cols), jnp.bfloat16),
            pltpu.VMEM((samples, steps, samples * micro, cols), jnp.bfloat16),
            pltpu.VMEM((chips, samples * micro, cols), jnp.float32),
            pltpu.VMEM((samples * micro, LANES), jnp.float32),
            pltpu.VMEM((steps, samples * micro, cols), jnp.bfloat16),
            pltpu.VMEM((samples, steps, micro, cols), jnp.bfloat16),
            pltpu.VMEM((samples, 8, rows), jnp.float32),
            pltpu.VMEM((steps, samples * micro, LANES), jnp.bfloat16),
            pltpu.VMEM((rows, LANES), jnp.float32),
            dma((peers, steps)),
            dma((peers, steps)),
            dma((chips, steps)),
            dma((chips, steps)),
            dma((steps,)),
            dma((steps,)),
            dma((chips, steps)),
            dma((chips, steps)),
            dma((samples - 1,)),
            dma((samples - 1,)),
            dma((peers, pieces)),
            dma((peers, pieces)),
            dma((steps,)),
            dma((steps,)),
        ],
        compiler_params=pltpu.CompilerParams(
            collective_id=0, has_side_effects=True, vmem_limit_bytes=56 * 2**20
        ),
        cost_estimate=pl.CostEstimate(
            flops=4 * rows * bond * bond, bytes_accessed=8 * bond * bond, transcendentals=rows
        ),
    )(tensor, charges, fronts_in, outcomes)
    return fronts[None], logs


def solution(mesh):
    in_specs = (
        P(("groups", "site"), None, None, "sample"),
        P(("groups", "sample"), None),
        P(("groups", "site"), "sample"),
        P("groups", None),
    )
    out_specs = (P(("groups", "site"), "sample", None), P(("groups", "site"), "sample"))
    return jax.shard_map(
        per_device, mesh=mesh, in_specs=in_specs, out_specs=out_specs, check_vma=False
    )
```

profile of v0, /device:TPU:17, one launch (start us, length us, event | category | flops | bytes accessed | tf_op | source)
XLA Modules:
  0.0 107.5 jit_solution(9875413870499756358)
XLA Ops:
  0.6 4.8 %copy.8 = bf16[1,2048,2,512]{3,1,2,0:T(8,128)(2,1)} copy(bf16[1,2048,2,512]{3,2,1,0:T(2,128)(2,1)} %param.4) | data formatting | bytes 8388608 | tf_op args[0]
  5.4 98.8 %shard_map.59 = (bf16[384,2048]{1,0:T(8,128)(2,1)}, f32[1,384]{1,0:T(1,128)}) custom-call(bf16[2,2048,512]{2,1,0:T(8,128)(2,1)} %bitcast.6, s32[5,16]{1,0:T(8,128)} %charges_ref.1, bf16[384,2048]{1,0:T(8,128)(2,1)} %fronts_ref.1, s32[1,384]{1,0:T(1,128)} %picks_ref.1), custom_call_target="tpu_custom_call" | custom-call | flops 6442450944 | bytes 33554432 | tf_op jit(solution)/shard_map/pallas_call | solution.py:431
  104.2 0.0 copy-start
  104.2 2.7 %copy.11 = bf16[1,384,2048]{2,1,0:T(8,128)(2,1)} copy(bf16[1,384,2048]{2,1,0:T(8,128)(2,1)} %bitcast.7) | data formatting | bytes 3145728
  106.9 0.0 copy-done
  106.9 0.6 copy.12
Async XLA Ops:
  104.2 2.7 %copy-start = (f32[1,384]{1,0:T(1,128)S(1)}, f32[1,384]{1,0:T(1,128)}, u32[]{:S(2)}) copy-start(f32[1,384]{1,0:T(1,128)} %get-tuple-element.9) | copy-start | bytes 4612
where the time goes:
time: 108 us; the launch traced here: 107 us
  Pallas kernels  98.8 us (91%)
  local copies, waits for them, and re-layouts  8.09 us (7%)
    pallas_call x1, Pallas kernels, per_device(): pl.pallas_call(functools.partial(chain_kernel, chips, sites, micro, piece...  98.8 us
    unnamed x5, local copies, waits for them, and re-layouts  8.09 us

commit v1 on v0

--- a/solution.py
+++ b/solution.py
@@ -164,7 +164,8 @@
                 full[o, b, pl.ds(pl.multiple_of(me * micro, SUB), micro), :] = fronts_ref[
                     b * micro : (b + 1) * micro, o * cols : (o + 1) * cols
                 ]
-        launch(0)
+        for b in range(min(2, steps)):
+            launch(b)
 
     def expand(owner, load, save, first, last):
         def body(i, carry):
@@ -216,9 +217,10 @@
         for j in range(rows // LANES):
             line = marks[o, 0:1, j * LANES : (j + 1) * LANES]
             square = jnp.broadcast_to(line, (LANES, LANES)).T.astype(jnp.bfloat16)
-            for q in range(LANES // micro):
-                columns[j * (LANES // micro) + q, o * micro : (o + 1) * micro, :] = square[
-                    q * micro : (q + 1) * micro, :
+            for q in range(LANES // SUB):
+                b, at = divmod(j * LANES + q * SUB, micro)
+                columns[b, o * micro + at : o * micro + at + SUB, :] = square[
+                    q * SUB : (q + 1) * SUB, :
                 ]
 
     @pl.when(is_tail)
@@ -241,22 +243,30 @@
         z_copy(0).wait_recv()
         launch(0)
 
-    first = jnp.where(site == 0, 1.0, 0.0)
+    def forward(b):
+        for d in range(1, chips):
+            x_copy(by_rows, behind(d, core), d, b, chip).wait_recv()
+            s_copy(by_rows, behind(d, core), d, b).start()
+
+    @pl.when(site == 0)
+    def _():
+        forward(0)
 
     chip_rows = pl.ds(pl.multiple_of(chip * pair, SUB), pair)
 
-    def contract(b, c, start, last):
+    def contract(b, c, start, last, norms=True):
         if last:
             front, picks, count = full[c, b, chip_rows, :], columns[b, chip_rows, :], pair
         else:
             front, picks, count = full[c, b], columns[b], samples * micro
         second = front * jnp.concatenate([picks] * (cols // LANES), axis=1)
         both = jnp.concatenate([front - second, second], axis=1)
-        total = jnp.zeros((count, LANES), jnp.float32)
-        for k in range(cols // LANES):
-            wide = front[:, k * LANES : (k + 1) * LANES].astype(jnp.float32)
-            total = total + wide * wide
-        sums[0:count, :] = total if start else sums[0:count, :] + total
+        if norms:
+            total = jnp.zeros((count, LANES), jnp.float32)
+            for k in range(cols // LANES):
+                wide = front[:, k * LANES : (k + 1) * LANES].astype(jnp.float32)
+                total = total + wide * wide
+            sums[0:count, :] = total if start else sums[0:count, :] + total
         for d in range(chips if last else 1):
             right = wf[c] if d == 0 else wx[d - 1, c]
             part = jnp.dot(both, right, preferred_element_type=jnp.float32)
@@ -264,8 +274,7 @@
 
     def scale_of(count):
         mean = jnp.sum(sums[0:count, :], axis=1, keepdims=True) * (1.0 / bond)
-        inverse = 1.0 / jnp.sqrt(mean + epsilon)
-        return inverse + first * (1.0 - inverse)
+        return 1.0 / jnp.sqrt(mean + epsilon)
 
     def finish(b):
         total = jnp.zeros((micro, LANES), jnp.float32)
@@ -302,6 +311,8 @@
             s_copy(block, behind(d, core), d, b).start()
             contract(b, behind(d, core), False, last)
             s_copy(block, behind(d, 1 - core), d, b).wait_recv()
+            if d == chips - 1:
+                b_copy(b).start()
             contract(b, behind(d, 1 - core), False, last)
 
     def step(b, carry):
@@ -313,23 +324,29 @@
         def _():
             early(b, by_chip, True)
 
-        @pl.when(b + 1 < steps)
-        def _():
-            @pl.when(site > 0)
-            def _():
-                z_copy(b + 1).wait_recv()
-
+        @pl.when((site > 0) & (b + 1 < steps))
+        def _():
+            z_copy(b + 1).wait_recv()
             launch(b + 1)
 
+        @pl.when((site == 0) & (b + 2 < steps))
+        def _():
+            launch(b + 2)
+
         @pl.when(site == 0)
         def _():
-            for d in range(1, chips):
-                x_copy(by_rows, behind(d, core), d, b, chip).wait_recv()
-                s_copy(by_rows, behind(d, core), d, b).start()
             for d in range(chips):
                 s_copy(by_rows, behind(d, 1 - core), d, b).wait_recv()
-            for c in range(samples):
-                contract(b, c, c == 0, False)
+            for c in range(samples - 1):
+                contract(b, c, c == 0, False, False)
+
+            @pl.when(b + 1 < steps)
+            def _():
+                forward(b + 1)
+
+            contract(b, samples - 1, False, False, False)
+            ybuf[b] = acc[0].astype(jnp.bfloat16)
+            z_copy(b).start()
 
         @pl.when((site > 0) & (site < tail))
         def _():
@@ -339,7 +356,7 @@
         def _():
             late(b, by_chip, True)
 
-        @pl.when(is_body)
+        @pl.when((site > 0) & (site < tail))
         def _():
             ybuf[b] = (acc[0] * scale_of(samples * micro)).astype(jnp.bfloat16)
             z_copy(b).start()
@@ -354,10 +371,6 @@
                 t_copy(d, b).start()
                 gath[behind(d, core), b] = ybuf[b, t_rows(d, b, core), :]
 
-        @pl.when(site > 0)
-        def _():
-            b_copy(b).start()
-
         @pl.when(is_tail & (b > 0))
         def _():
             finish_tail(b - 1)
@@ -412,6 +425,16 @@
         return carry
 
     lax.fori_loop(0, steps, drain, 0)
+
+
+def micro_rows(rows):
+    best = rows
+    for count in range(1, rows // SUB + 1):
+        if rows % count == 0 and (rows // count) % SUB == 0:
+            best = rows // count
+            if count >= 8:
+                break
+    return best
 
 
 def per_device(site_tensor, fronts_in, outcomes, charges):
@@ -423,7 +446,7 @@
     tensor = site_tensor[0].transpose(1, 0, 2)
     pieces = 4
 
-    micro = 32
+    micro = micro_rows(rows)
     steps = rows // micro
     vmem = pl.BlockSpec(memory_space=pltpu.VMEM)
     dma = pltpu.SemaphoreType.DMA
@@ -465,7 +488,7 @@
             dma((steps,)),
         ],
         compiler_params=pltpu.CompilerParams(
-            collective_id=0, has_side_effects=True, vmem_limit_bytes=56 * 2**20
+            collective_id=0, has_side_effects=True, vmem_limit_bytes=36 * 2**20
         ),
         cost_estimate=pl.CostEstimate(
             flops=4 * rows * bond * bond, bytes_accessed=8 * bond * bond, transcendentals=rows

time: 108 us -> 98.3 us (0.910)
  Pallas kernels: 98.8 us -> 92.7 us
  local copies, waits for them, and re-layouts: 8.09 us -> 4.7 us
    pallas_call x1, Pallas kernels: 98.8 us -> 92.7 us  [per_device(): pl.pallas_call(functools.partial(chain_kernel, chips, sites, micro, piece...]
    unnamed x5 -> x9, local copies, waits for them, and re-layouts: 8.09 us -> 4.7 us
where the time goes in v1:
time: 98.3 us; the launch traced here: 98.1 us
  Pallas kernels  92.7 us (94%)
  local copies, waits for them, and re-layouts  4.7 us (5%)
    pallas_call x1, Pallas kernels, per_device(): pl.pallas_call(functools.partial(chain_kernel, chips, sites, micro, piece...  92.7 us
    unnamed x9, local copies, waits for them, and re-layouts  4.7 us

profile of v1, /device:TPU:17, one launch (start us, length us, event | category | flops | bytes accessed | tf_op | source)
XLA Modules:
  0.0 98.1 jit_solution(2025978832454038661)
XLA Ops:
  0.6 0.0 copy-start.1
  0.6 0.0 copy-start.2
  0.7 0.0 copy-start
  0.7 3.0 %copy.8 = bf16[1,2048,2,512]{3,1,2,0:T(8,128)(2,1)S(1)} copy(bf16[1,2048,2,512]{3,2,1,0:T(2,128)(2,1)} %param.4) | data formatting | bytes 8388608 | tf_op args[0]
  3.6 0.0 copy-done.1
  3.7 0.0 copy-done.2
  3.7 0.0 copy-done
  3.7 92.7 %shard_map.59 = (bf16[384,2048]{1,0:T(8,128)(2,1)S(1)}, f32[1,384]{1,0:T(1,128)S(1)}) custom-call(bf16[2,2048,512]{2,1,0:T(8,128)(2,1)S(1)} %bitcast.6, s32[5,16]{1,0:T(8,128)S(1)} %copy-done.1, bf16[384,2048]{1,0:T(8,128)(2,1)S(1)} %copy-done, s32[1,384]{1,0:T(1,128)S(1)} %copy-done.2), custom_call_target="tpu_custom_call" | custom-call | flops 6442450944 | bytes 33554432 | tf_op jit(solution)/shard_map/pallas_call | solution.py:454
  96.4 1.1 %copy.11 = bf16[1,384,2048]{2,1,0:T(8,128)(2,1)} copy(bf16[1,384,2048]{2,1,0:T(8,128)(2,1)S(1)} %bitcast.7) | data formatting | bytes 3145728
  97.6 0.6 copy.12
Async XLA Ops:
  0.6 3.0 %copy-start.1 = (s32[5,16]{1,0:T(8,128)S(1)}, s32[5,16]{1,0:T(8,128)}, u32[]{:S(2)}) copy-start(s32[5,16]{1,0:T(8,128)} %charges_ref.1) | copy-start | bytes 964
  0.6 3.0 %copy-start.2 = (s32[1,384]{1,0:T(1,128)S(1)}, s32[1,384]{1,0:T(1,128)}, u32[]{:S(2)}) copy-start(s32[1,384]{1,0:T(1,128)} %picks_ref.1) | copy-start | bytes 4612
  0.7 3.0 %copy-start = (bf16[384,2048]{1,0:T(8,128)(2,1)S(1)}, bf16[384,2048]{1,0:T(8,128)(2,1)}, u32[]{:S(2)}) copy-start(bf16[384,2048]{1,0:T(8,128)(2,1)} %fronts_ref.1) | copy-start | bytes 4718596

commit v2 on v1

--- a/solution.py
+++ b/solution.py
@@ -125,12 +125,23 @@
             {"site": jnp.minimum(site + 1, sites - 1)},
         )
 
-    def b_copy(b):
-        return remote(
-            full.at[:, b, pl.ds(pl.multiple_of(me * micro, SUB), micro), :],
-            gath.at[:, b], b_send.at[b], b_recv.at[b],
+    def b_copy(d, b):
+        there = pl.ds(behind(d, 0), 2)
+        return remote(
+            full.at[there, b, pl.ds(pl.multiple_of(me * micro, SUB), micro), :],
+            gath.at[there, b], b_send.at[d - 1, b], b_recv.at[d - 1, b],
             {"site": jnp.maximum(site - 1, 0)},
         )
+
+    def u_copy(b):
+        return remote(
+            ybuf.at[b, pl.ds(pl.multiple_of(sibling * micro, SUB), micro), :],
+            gath.at[me, b], a_send.at[0, b], a_recv.at[0, b], {"sample": sibling},
+        )
+
+    def u_arrival(b):
+        slot = gath.at[sibling, b]
+        return remote(slot, slot, a_send.at[0, b], a_recv.at[0, b], {"sample": sibling})
 
     def p_copy(e):
         target = lax.rem(me + e, samples)
@@ -291,7 +302,10 @@
             out_ref[span, c * cols : (c + 1) * cols] = (wide * inverse).astype(jnp.bfloat16)
 
     def finish_body(b, carry):
-        b_copy(b).wait_recv()
+        gath[me, b] = ybuf[b, pl.ds(pl.multiple_of(me * micro, SUB), micro), :]
+        u_arrival(b).wait_recv()
+        for d in range(1, chips):
+            b_copy(d, b).wait_recv()
         finish(b)
         return carry
 
@@ -311,8 +325,7 @@
             s_copy(block, behind(d, core), d, b).start()
             contract(b, behind(d, core), False, last)
             s_copy(block, behind(d, 1 - core), d, b).wait_recv()
-            if d == chips - 1:
-                b_copy(b).start()
+            b_copy(d, b).start()
             contract(b, behind(d, 1 - core), False, last)
 
     def step(b, carry):
@@ -347,6 +360,7 @@
             contract(b, samples - 1, False, False, False)
             ybuf[b] = acc[0].astype(jnp.bfloat16)
             z_copy(b).start()
+            u_copy(b).start()
 
         @pl.when((site > 0) & (site < tail))
         def _():
@@ -360,6 +374,7 @@
         def _():
             ybuf[b] = (acc[0] * scale_of(samples * micro)).astype(jnp.bfloat16)
             z_copy(b).start()
+            u_copy(b).start()
 
         @pl.when(is_tail)
         def _():
@@ -411,7 +426,12 @@
 
         @pl.when(site > 0)
         def _():
-            b_copy(b).wait_send()
+            for d in range(1, chips):
+                b_copy(d, b).wait_send()
+
+        @pl.when(is_body)
+        def _():
+            u_copy(b).wait_send()
 
         @pl.when(is_tail)
         def _():
@@ -484,8 +504,8 @@
             dma((samples - 1,)),
             dma((peers, pieces)),
             dma((peers, pieces)),
-            dma((steps,)),
-            dma((steps,)),
+            dma((peers, steps)),
+            dma((peers, steps)),
         ],
         compiler_params=pltpu.CompilerParams(
             collective_id=0, has_side_effects=True, vmem_limit_bytes=36 * 2**20

time: 98.3 us -> 93.4 us (0.950)
  Pallas kernels: 92.7 us -> 87.9 us
    pallas_call x1, Pallas kernels: 92.7 us -> 87.9 us  [per_device(): pl.pallas_call(functools.partial(chain_kernel, chips, sites, micro, piece...]
where the time goes in v2:
time: 93.4 us; the launch traced here: 93.3 us
  Pallas kernels  87.9 us (94%)
  local copies, waits for them, and re-layouts  4.7 us (5%)
    pallas_call x1, Pallas kernels, per_device(): pl.pallas_call(functools.partial(chain_kernel, chips, sites, micro, piece...  87.9 us
    unnamed x9, local copies, waits for them, and re-layouts  4.7 us

profile of v2, /device:TPU:17, one launch (start us, length us, event | category | flops | bytes accessed | tf_op | source)
XLA Modules:
  0.0 93.3 jit_solution(9648266155310274580)
XLA Ops:
  0.6 0.0 copy-start.1
  0.6 0.0 copy-start.2
  0.7 0.0 copy-start
  0.7 3.0 %copy.8 = bf16[1,2048,2,512]{3,1,2,0:T(8,128)(2,1)S(1)} copy(bf16[1,2048,2,512]{3,2,1,0:T(2,128)(2,1)} %param.4) | data formatting | bytes 8388608 | tf_op args[0]
  3.6 0.0 copy-done.1
  3.7 0.0 copy-done.2
  3.7 0.0 copy-done
  3.7 87.9 %shard_map.59 = (bf16[384,2048]{1,0:T(8,128)(2,1)S(1)}, f32[1,384]{1,0:T(1,128)S(1)}) custom-call(bf16[2,2048,512]{2,1,0:T(8,128)(2,1)S(1)} %bitcast.6, s32[5,16]{1,0:T(8,128)S(1)} %copy-done.1, bf16[384,2048]{1,0:T(8,128)(2,1)S(1)} %copy-done, s32[1,384]{1,0:T(1,128)S(1)} %copy-done.2), custom_call_target="tpu_custom_call" | custom-call | flops 6442450944 | bytes 33554432 | tf_op jit(solution)/shard_map/pallas_call | solution.py:474
  91.6 1.1 %copy.11 = bf16[1,384,2048]{2,1,0:T(8,128)(2,1)} copy(bf16[1,384,2048]{2,1,0:T(8,128)(2,1)S(1)} %bitcast.7) | data formatting | bytes 3145728
  92.7 0.6 copy.12
Async XLA Ops:
  0.6 3.0 %copy-start.1 = (s32[5,16]{1,0:T(8,128)S(1)}, s32[5,16]{1,0:T(8,128)}, u32[]{:S(2)}) copy-start(s32[5,16]{1,0:T(8,128)} %charges_ref.1) | copy-start | bytes 964
  0.6 3.0 %copy-start.2 = (s32[1,384]{1,0:T(1,128)S(1)}, s32[1,384]{1,0:T(1,128)}, u32[]{:S(2)}) copy-start(s32[1,384]{1,0:T(1,128)} %picks_ref.1) | copy-start | bytes 4612
  0.7 3.0 %copy-start = (bf16[384,2048]{1,0:T(8,128)(2,1)S(1)}, bf16[384,2048]{1,0:T(8,128)(2,1)}, u32[]{:S(2)}) copy-start(bf16[384,2048]{1,0:T(8,128)(2,1)} %fronts_ref.1) | copy-start | bytes 4718596
